TPU v7x, 256 devices: a whole 4x4x8 slice. The times are simulated.
256 devices in a mesh: ctx: 64 (over y, z, x_lo), head: 4 (over x_hi, core).
Axes of the slice: x: 4 (x_hi: 2, x_lo: 2; x = x_hi * 2 + x_lo), y: 4, z: 8, core: 2. Of those that a mesh axis runs over, the one named last changes fastest.
Arguments:
- queries: bfloat16 [16384, 2048], P('ctx', 'head'), may hold values from -32 to 32
- keys: bfloat16 [16384, 1024], P('ctx', 'head'), may hold values from -32 to 32
- values: bfloat16 [16384, 1024], P('ctx', 'head'), may hold values from -6 to 6
- doc_ids: int32 [128], replicated, may hold values from 0 to 7, as said below
- out_weight: bfloat16 [2048, 5376], P('head'), may hold values from -1 to 1
Outputs:
- projected: bfloat16 [16384, 5376], P(('ctx', 'head'))
Inputs may be any that keep to these rules, and one draw needn't show every extreme that they name: doc_ids is non-decreasing along the sequence and starts at 0; the first document spans exactly 96 blocks, every other one 1 or more blocks.
All inputs are finite; a program needn't handle non-finite values.
Results may differ from a plain program's by a relative error of at most 0.015.
Values may be sent and summed in bfloat16 or wider, within the bound.
A program may use at most 64 MiB of HBM per device.

v0:
```python
import jax
import jax.numpy as jnp
from jax import lax
from jax.sharding import PartitionSpec as P

HEAD_SIZE = 128
BLOCK = 128


SCALE = 168.0 ** (-0.5)
NEG = -1e30


def from_behind(block, axis, distance):
    devices = range(lax.axis_size(axis))
    route = [(i - distance, i) for i in devices if i - distance in devices]
    return lax.ppermute(block, axis, route)


def token_docs(doc_ids, start, count):
    blocks = (start + jnp.arange(count, dtype=jnp.int32)) // BLOCK
    table = blocks[:, None] == jnp.arange(doc_ids.shape[0], dtype=jnp.int32)[None, :]
    return jnp.sum(jnp.where(table, doc_ids[None, :], 0), axis=1)


def attend(carry, queries, q_docs, q_start, k_piece, v_piece, k_docs, k_start):
    peak, totals, accum = carry
    n_query = queries.shape[0]
    n_key = k_piece.shape[0]
    kv_heads = k_piece.shape[1] // HEAD_SIZE
    query_group = queries.shape[1] // k_piece.shape[1]
    q_heads = queries.reshape(n_query, kv_heads, query_group, HEAD_SIZE)
    k_heads = k_piece.reshape(n_key, kv_heads, HEAD_SIZE)
    v_heads = v_piece.reshape(n_key, kv_heads, HEAD_SIZE)
    scores = (
        jnp.einsum("qkgd,skd->kgqs", q_heads, k_heads, preferred_element_type=jnp.float32) * SCALE
    )
    q_pos = q_start + jnp.arange(n_query, dtype=jnp.int32)
    k_pos = k_start + jnp.arange(n_key, dtype=jnp.int32)
    allowed = (q_docs[:, None] == k_docs[None, :]) & (q_pos[:, None] >= k_pos[None, :])
    scores = jnp.where(allowed, scores, NEG)
    new_peak = jnp.maximum(peak, jnp.max(scores, axis=-1))
    shrink = jnp.exp(peak - new_peak)
    weights = jnp.exp(scores - new_peak[..., None])
    totals = totals * shrink + jnp.sum(weights, axis=-1)
    rounded = weights.astype(jnp.bfloat16)
    added = jnp.einsum("kgqs,skd->kgqd", rounded, v_heads, preferred_element_type=jnp.float32)
    accum = accum * shrink[..., None] + added
    return (new_peak, totals, accum)


def absorb_block(carry, queries, q_docs, q_start, k_piece, v_piece, k_start, doc_ids, flag):
    n_key = k_piece.shape[0]
    k_docs = token_docs(doc_ids, k_start, n_key)
    fresh = attend(carry, queries, q_docs, q_start, k_piece, v_piece, k_docs, k_start)
    return jax.tree.map(lambda new, old: jnp.where(flag, new, old), fresh, carry)


def per_device(queries, keys, values, doc_ids, out_weight):
    n_ctx = lax.axis_size("ctx")
    position = lax.axis_index("ctx")
    n_query = queries.shape[0]
    q_start = position * n_query
    q_docs = token_docs(doc_ids, q_start, n_query)
    kv_heads = keys.shape[1] // HEAD_SIZE
    query_group = queries.shape[1] // keys.shape[1]
    carry = (
        jnp.full((kv_heads, query_group, n_query), NEG, jnp.float32),
        jnp.zeros((kv_heads, query_group, n_query), jnp.float32),
        jnp.zeros((kv_heads, query_group, n_query, HEAD_SIZE), jnp.float32),
    )
    always = jnp.array(True)
    carry = absorb_block(carry, queries, q_docs, q_start, keys, values, q_start, doc_ids, always)
    stacked = jnp.stack((keys, values))
    span = n_ctx - 1

    def turn_one(step, state):
        inner_state, moving = state
        moving = from_behind(moving, "ctx", 1)
        source = (position - step) % n_ctx
        inner_state = absorb_block(
            inner_state,
            queries,
            q_docs,
            q_start,
            moving[0],
            moving[1],
            source * n_query,
            doc_ids,
            always,
        )
        return (inner_state, moving)

    carry = lax.fori_loop(1, span + 1, turn_one, (carry, stacked))[0]
    peak, totals, accum = carry
    result = accum / totals[..., None]
    attended = (
        jnp.transpose(result, (2, 0, 1, 3)).reshape(n_query, queries.shape[1]).astype(jnp.bfloat16)
    )
    return lax.psum_scatter(
        jnp.dot(attended, out_weight, preferred_element_type=jnp.float32).astype(jnp.bfloat16),
        "head",
        scatter_dimension=0,
        tiled=True,
    )


def solution(mesh):
    placed = (P("ctx", "head"), P("ctx", "head"), P("ctx", "head"), P(), P("head", None))
    return jax.shard_map(
        per_device, mesh=mesh, in_specs=placed, out_specs=P(("ctx", "head"), None), check_vma=False
    )
```

profile of v0, /device:TPU:1, one launch (start us, length us, event | category | flops | bytes accessed | tf_op | source)
XLA Modules:
  0.0 898.1 jit_solution(3215895118319566616)
XLA Ops:
  14.5 699.4 %while.22 = (s32[]{:T(128)}, f32[2,2,256]{2,1,0:T(2,128)S(1)}, f32[2,2,256]{2,1,0:T(2,128)S(1)}, f32[2,2,256,128]{3,2,1,0:T(8,128)S(1)}, bf16[2,256,256]{1,2,0:T...) while((s32[]{:T(128)}, f32[2,2,256]{2,1,0:T(2,128)S(1)}, ...), condition=%wide.wide.region_7.8_spmd, body=%wide.wide.region_3.7_spmd.sunk | while | flops 136616208 | bytes 7022414 | solution.py:94
  42.7 5.0 collective-permute-start
  79.7 4.8 collective-permute-start
  89.7 5.0 collective-permute-start
  95.1 4.8 collective-permute-done
  101.1 5.0 collective-permute-start
  106.5 5.4 collective-permute-done
  123.3 5.0 collective-permute-start
  133.2 5.0 collective-permute-start
  142.6 5.0 collective-permute-start
  152.1 5.6 collective-permute-start
  162.2 7.1 collective-permute-start
  173.7 5.0 collective-permute-start
  183.2 5.1 collective-permute-start
  192.7 6.2 collective-permute-start
  203.4 6.2 collective-permute-start
  214.1 6.2 collective-permute-start
  225.3 6.2 collective-permute-start
  237.6 6.6 collective-permute-start
  244.6 5.7 collective-permute-done
  251.4 6.7 collective-permute-start
  264.2 6.4 collective-permute-start
  275.6 6.2 collective-permute-start
  286.2 5.1 collective-permute-start
  295.8 5.7 collective-permute-start
  315.1 6.2 collective-permute-start
  325.7 6.2 collective-permute-start
  336.4 6.3 collective-permute-start
  348.0 6.4 collective-permute-start
  360.6 6.8 collective-permute-start
  367.7 5.6 collective-permute-done
  374.4 6.6 collective-permute-start
  386.9 6.7 collective-permute-start
  398.5 5.3 collective-permute-start
  408.2 5.4 collective-permute-start
  418.1 5.8 collective-permute-start
  428.3 5.6 collective-permute-start
  438.4 6.2 collective-permute-start
  449.1 6.2 collective-permute-start
  459.8 6.3 collective-permute-start
  471.3 6.4 collective-permute-start
  478.1 4.7 collective-permute-done
  484.0 6.8 collective-permute-start
  491.2 5.5 collective-permute-done
  508.6 5.0 collective-permute-start
  518.7 5.0 collective-permute-start
  528.1 7.6 collective-permute-start
  540.4 11.2 %collective-permute-start = (bf16[2,256,256]{1,2,0:T(8,128)(2,1)S(1)}, bf16[2,256,256]{1,2,0:T(8,128)(2,1)S(1)}, u32[]{:S(2)}, u32[]{:S(2)}) collective-permute-start(bf16[2,256,256]{1,2,0:T(8,128)(2,1)S(1)} %get-tuple-element.438), channel_id=1, source_target_pairs={{0,4},{4,8},{8,12},{12,16},{16,20},{20,24},{24,28},{28,32},{32,36}... | collective-permute-start | bytes 786440 | tf_op jit(solution)/shard_map/while/body/eval_jaxpr/ppermute | solution.py:17
  557.6 5.3 collective-permute-start
  568.1 8.0 collective-permute-start
  580.9 7.1 collective-permute-start
  592.5 7.4 collective-permute-start
  604.3 7.3 collective-permute-start
  616.1 6.4 collective-permute-start
  626.9 6.8 collective-permute-start
  638.2 7.4 collective-permute-start
  650.0 6.3 collective-permute-start
  661.2 6.7 collective-permute-start
  673.5 7.7 collective-permute-start
  681.6 5.4 collective-permute-done
  688.1 8.4 collective-permute-start
  702.4 6.1 collective-permute-start
  714.2 5.7 convolution_convert_fusion
  719.9 171.4 %reduce-scatter.2.cloned.1.call-done = bf16[64,5376]{1,0:T(8,128)(2,1)} async-done(((bf16[256,5376]{1,0:T(8,128)(2,1)}), bf16[64,5376]{1,0:T(8,128)(2,1)}) %reduce-scatter.2.cloned.1.call-update) | async-done | bytes 688144 | tf_op jit(solution)/shard_map/reduce_scatter | solution.py:100
  (842 shorter events, 325.6 us)
Async XLA Ops:
  6.5 884.8 %reduce-scatter.2.cloned.1.call-start = ((), (), s32[]{:S(2)}) async-start(), calls=%async_computation.1 | async-start | bytes 3440640 | tf_op jit(solution)/shard_map/reduce_scatter | solution.py:100
  14.5 8.9 collective-permute-start
  24.6 8.1 collective-permute-start
  33.9 7.7 collective-permute-start
  42.7 8.3 collective-permute-start
  52.2 8.0 collective-permute-start
  61.4 8.0 collective-permute-start
  70.5 8.0 collective-permute-start
  79.7 8.9 collective-permute-start
  89.7 10.2 %collective-permute-start = (bf16[2,256,256]{1,2,0:T(8,128)(2,1)S(1)}, bf16[2,256,256]{1,2,0:T(8,128)(2,1)S(1)}, u32[]{:S(2)}, u32[]{:S(2)}) collective-permute-start(bf16[2,256,256]{1,2,0:T(8,128)(2,1)S(1)} %get-tuple-element.438), channel_id=1, source_target_pairs={{0,4},{4,8},{8,12},{12,16},{16,20},{20,24},{24,28},{28,32},{32,36}... | collective-permute-start | bytes 786440 | tf_op jit(solution)/shard_map/while/body/eval_jaxpr/ppermute | solution.py:17
  101.1 10.8 %collective-permute-start = (bf16[2,256,256]{1,2,0:T(8,128)(2,1)S(1)}, bf16[2,256,256]{1,2,0:T(8,128)(2,1)S(1)}, u32[]{:S(2)}, u32[]{:S(2)}) collective-permute-start(bf16[2,256,256]{1,2,0:T(8,128)(2,1)S(1)} %get-tuple-element.438), channel_id=1, source_target_pairs={{0,4},{4,8},{8,12},{12,16},{16,20},{20,24},{24,28},{28,32},{32,36}... | collective-permute-start | bytes 786440 | tf_op jit(solution)/shard_map/while/body/eval_jaxpr/ppermute | solution.py:17
  113.1 9.1 %collective-permute-start = (bf16[2,256,256]{1,2,0:T(8,128)(2,1)S(1)}, bf16[2,256,256]{1,2,0:T(8,128)(2,1)S(1)}, u32[]{:S(2)}, u32[]{:S(2)}) collective-permute-start(bf16[2,256,256]{1,2,0:T(8,128)(2,1)S(1)} %get-tuple-element.438), channel_id=1, source_target_pairs={{0,4},{4,8},{8,12},{12,16},{16,20},{20,24},{24,28},{28,32},{32,36}... | collective-permute-start | bytes 786440 | tf_op jit(solution)/shard_map/while/body/eval_jaxpr/ppermute | solution.py:17
  123.3 8.7 collective-permute-start
  133.2 8.3 collective-permute-start
  142.6 8.3 collective-permute-start
  152.1 8.9 collective-permute-start
  162.2 10.4 %collective-permute-start = (bf16[2,256,256]{1,2,0:T(8,128)(2,1)S(1)}, bf16[2,256,256]{1,2,0:T(8,128)(2,1)S(1)}, u32[]{:S(2)}, u32[]{:S(2)}) collective-permute-start(bf16[2,256,256]{1,2,0:T(8,128)(2,1)S(1)} %get-tuple-element.438), channel_id=1, source_target_pairs={{0,4},{4,8},{8,12},{12,16},{16,20},{20,24},{24,28},{28,32},{32,36}... | collective-permute-start | bytes 786440 | tf_op jit(solution)/shard_map/while/body/eval_jaxpr/ppermute | solution.py:17
  173.7 8.3 collective-permute-start
  183.2 8.4 collective-permute-start
  192.7 9.5 %collective-permute-start = (bf16[2,256,256]{1,2,0:T(8,128)(2,1)S(1)}, bf16[2,256,256]{1,2,0:T(8,128)(2,1)S(1)}, u32[]{:S(2)}, u32[]{:S(2)}) collective-permute-start(bf16[2,256,256]{1,2,0:T(8,128)(2,1)S(1)} %get-tuple-element.438), channel_id=1, source_target_pairs={{0,4},{4,8},{8,12},{12,16},{16,20},{20,24},{24,28},{28,32},{32,36}... | collective-permute-start | bytes 786440 | tf_op jit(solution)/shard_map/while/body/eval_jaxpr/ppermute | solution.py:17
  203.4 9.5 %collective-permute-start = (bf16[2,256,256]{1,2,0:T(8,128)(2,1)S(1)}, bf16[2,256,256]{1,2,0:T(8,128)(2,1)S(1)}, u32[]{:S(2)}, u32[]{:S(2)}) collective-permute-start(bf16[2,256,256]{1,2,0:T(8,128)(2,1)S(1)} %get-tuple-element.438), channel_id=1, source_target_pairs={{0,4},{4,8},{8,12},{12,16},{16,20},{20,24},{24,28},{28,32},{32,36}... | collective-permute-start | bytes 786440 | tf_op jit(solution)/shard_map/while/body/eval_jaxpr/ppermute | solution.py:17
  214.1 10.0 %collective-permute-start = (bf16[2,256,256]{1,2,0:T(8,128)(2,1)S(1)}, bf16[2,256,256]{1,2,0:T(8,128)(2,1)S(1)}, u32[]{:S(2)}, u32[]{:S(2)}) collective-permute-start(bf16[2,256,256]{1,2,0:T(8,128)(2,1)S(1)} %get-tuple-element.438), channel_id=1, source_target_pairs={{0,4},{4,8},{8,12},{12,16},{16,20},{20,24},{24,28},{28,32},{32,36}... | collective-permute-start | bytes 786440 | tf_op jit(solution)/shard_map/while/body/eval_jaxpr/ppermute | solution.py:17
  225.3 11.2 %collective-permute-start = (bf16[2,256,256]{1,2,0:T(8,128)(2,1)S(1)}, bf16[2,256,256]{1,2,0:T(8,128)(2,1)S(1)}, u32[]{:S(2)}, u32[]{:S(2)}) collective-permute-start(bf16[2,256,256]{1,2,0:T(8,128)(2,1)S(1)} %get-tuple-element.438), channel_id=1, source_target_pairs={{0,4},{4,8},{8,12},{12,16},{16,20},{20,24},{24,28},{28,32},{32,36}... | collective-permute-start | bytes 786440 | tf_op jit(solution)/shard_map/while/body/eval_jaxpr/ppermute | solution.py:17
  237.6 12.7 %collective-permute-start = (bf16[2,256,256]{1,2,0:T(8,128)(2,1)S(1)}, bf16[2,256,256]{1,2,0:T(8,128)(2,1)S(1)}, u32[]{:S(2)}, u32[]{:S(2)}) collective-permute-start(bf16[2,256,256]{1,2,0:T(8,128)(2,1)S(1)} %get-tuple-element.438), channel_id=1, source_target_pairs={{0,4},{4,8},{8,12},{12,16},{16,20},{20,24},{24,28},{28,32},{32,36}... | collective-permute-start | bytes 786440 | tf_op jit(solution)/shard_map/while/body/eval_jaxpr/ppermute | solution.py:17
  251.4 11.7 %collective-permute-start = (bf16[2,256,256]{1,2,0:T(8,128)(2,1)S(1)}, bf16[2,256,256]{1,2,0:T(8,128)(2,1)S(1)}, u32[]{:S(2)}, u32[]{:S(2)}) collective-permute-start(bf16[2,256,256]{1,2,0:T(8,128)(2,1)S(1)} %get-tuple-element.438), channel_id=1, source_target_pairs={{0,4},{4,8},{8,12},{12,16},{16,20},{20,24},{24,28},{28,32},{32,36}... | collective-permute-start | bytes 786440 | tf_op jit(solution)/shard_map/while/body/eval_jaxpr/ppermute | solution.py:17
  264.2 10.2 %collective-permute-start = (bf16[2,256,256]{1,2,0:T(8,128)(2,1)S(1)}, bf16[2,256,256]{1,2,0:T(8,128)(2,1)S(1)}, u32[]{:S(2)}, u32[]{:S(2)}) collective-permute-start(bf16[2,256,256]{1,2,0:T(8,128)(2,1)S(1)} %get-tuple-element.438), channel_id=1, source_target_pairs={{0,4},{4,8},{8,12},{12,16},{16,20},{20,24},{24,28},{28,32},{32,36}... | collective-permute-start | bytes 786440 | tf_op jit(solution)/shard_map/while/body/eval_jaxpr/ppermute | solution.py:17
  275.6 9.5 %collective-permute-start = (bf16[2,256,256]{1,2,0:T(8,128)(2,1)S(1)}, bf16[2,256,256]{1,2,0:T(8,128)(2,1)S(1)}, u32[]{:S(2)}, u32[]{:S(2)}) collective-permute-start(bf16[2,256,256]{1,2,0:T(8,128)(2,1)S(1)} %get-tuple-element.438), channel_id=1, source_target_pairs={{0,4},{4,8},{8,12},{12,16},{16,20},{20,24},{24,28},{28,32},{32,36}... | collective-permute-start | bytes 786440 | tf_op jit(solution)/shard_map/while/body/eval_jaxpr/ppermute | solution.py:17
  286.2 8.4 collective-permute-start
  295.8 9.0 %collective-permute-start = (bf16[2,256,256]{1,2,0:T(8,128)(2,1)S(1)}, bf16[2,256,256]{1,2,0:T(8,128)(2,1)S(1)}, u32[]{:S(2)}, u32[]{:S(2)}) collective-permute-start(bf16[2,256,256]{1,2,0:T(8,128)(2,1)S(1)} %get-tuple-element.438), channel_id=1, source_target_pairs={{0,4},{4,8},{8,12},{12,16},{16,20},{20,24},{24,28},{28,32},{32,36}... | collective-permute-start | bytes 786440 | tf_op jit(solution)/shard_map/while/body/eval_jaxpr/ppermute | solution.py:17
  305.9 8.0 collective-permute-start
  315.1 9.5 %collective-permute-start = (bf16[2,256,256]{1,2,0:T(8,128)(2,1)S(1)}, bf16[2,256,256]{1,2,0:T(8,128)(2,1)S(1)}, u32[]{:S(2)}, u32[]{:S(2)}) collective-permute-start(bf16[2,256,256]{1,2,0:T(8,128)(2,1)S(1)} %get-tuple-element.438), channel_id=1, source_target_pairs={{0,4},{4,8},{8,12},{12,16},{16,20},{20,24},{24,28},{28,32},{32,36}... | collective-permute-start | bytes 786440 | tf_op jit(solution)/shard_map/while/body/eval_jaxpr/ppermute | solution.py:17
  325.7 9.6 %collective-permute-start = (bf16[2,256,256]{1,2,0:T(8,128)(2,1)S(1)}, bf16[2,256,256]{1,2,0:T(8,128)(2,1)S(1)}, u32[]{:S(2)}, u32[]{:S(2)}) collective-permute-start(bf16[2,256,256]{1,2,0:T(8,128)(2,1)S(1)} %get-tuple-element.438), channel_id=1, source_target_pairs={{0,4},{4,8},{8,12},{12,16},{16,20},{20,24},{24,28},{28,32},{32,36}... | collective-permute-start | bytes 786440 | tf_op jit(solution)/shard_map/while/body/eval_jaxpr/ppermute | solution.py:17
  336.4 10.4 %collective-permute-start = (bf16[2,256,256]{1,2,0:T(8,128)(2,1)S(1)}, bf16[2,256,256]{1,2,0:T(8,128)(2,1)S(1)}, u32[]{:S(2)}, u32[]{:S(2)}) collective-permute-start(bf16[2,256,256]{1,2,0:T(8,128)(2,1)S(1)} %get-tuple-element.438), channel_id=1, source_target_pairs={{0,4},{4,8},{8,12},{12,16},{16,20},{20,24},{24,28},{28,32},{32,36}... | collective-permute-start | bytes 786440 | tf_op jit(solution)/shard_map/while/body/eval_jaxpr/ppermute | solution.py:17
  348.0 11.5 %collective-permute-start = (bf16[2,256,256]{1,2,0:T(8,128)(2,1)S(1)}, bf16[2,256,256]{1,2,0:T(8,128)(2,1)S(1)}, u32[]{:S(2)}, u32[]{:S(2)}) collective-permute-start(bf16[2,256,256]{1,2,0:T(8,128)(2,1)S(1)} %get-tuple-element.438), channel_id=1, source_target_pairs={{0,4},{4,8},{8,12},{12,16},{16,20},{20,24},{24,28},{28,32},{32,36}... | collective-permute-start | bytes 786440 | tf_op jit(solution)/shard_map/while/body/eval_jaxpr/ppermute | solution.py:17
  360.6 12.7 %collective-permute-start = (bf16[2,256,256]{1,2,0:T(8,128)(2,1)S(1)}, bf16[2,256,256]{1,2,0:T(8,128)(2,1)S(1)}, u32[]{:S(2)}, u32[]{:S(2)}) collective-permute-start(bf16[2,256,256]{1,2,0:T(8,128)(2,1)S(1)} %get-tuple-element.438), channel_id=1, source_target_pairs={{0,4},{4,8},{8,12},{12,16},{16,20},{20,24},{24,28},{28,32},{32,36}... | collective-permute-start | bytes 786440 | tf_op jit(solution)/shard_map/while/body/eval_jaxpr/ppermute | solution.py:17
  374.4 11.3 %collective-permute-start = (bf16[2,256,256]{1,2,0:T(8,128)(2,1)S(1)}, bf16[2,256,256]{1,2,0:T(8,128)(2,1)S(1)}, u32[]{:S(2)}, u32[]{:S(2)}) collective-permute-start(bf16[2,256,256]{1,2,0:T(8,128)(2,1)S(1)} %get-tuple-element.438), channel_id=1, source_target_pairs={{0,4},{4,8},{8,12},{12,16},{16,20},{20,24},{24,28},{28,32},{32,36}... | collective-permute-start | bytes 786440 | tf_op jit(solution)/shard_map/while/body/eval_jaxpr/ppermute | solution.py:17
  386.9 10.4 %collective-permute-start = (bf16[2,256,256]{1,2,0:T(8,128)(2,1)S(1)}, bf16[2,256,256]{1,2,0:T(8,128)(2,1)S(1)}, u32[]{:S(2)}, u32[]{:S(2)}) collective-permute-start(bf16[2,256,256]{1,2,0:T(8,128)(2,1)S(1)} %get-tuple-element.438), channel_id=1, source_target_pairs={{0,4},{4,8},{8,12},{12,16},{16,20},{20,24},{24,28},{28,32},{32,36}... | collective-permute-start | bytes 786440 | tf_op jit(solution)/shard_map/while/body/eval_jaxpr/ppermute | solution.py:17
  398.5 8.6 collective-permute-start
  408.2 8.7 collective-permute-start
  418.1 9.1 %collective-permute-start = (bf16[2,256,256]{1,2,0:T(8,128)(2,1)S(1)}, bf16[2,256,256]{1,2,0:T(8,128)(2,1)S(1)}, u32[]{:S(2)}, u32[]{:S(2)}) collective-permute-start(bf16[2,256,256]{1,2,0:T(8,128)(2,1)S(1)} %get-tuple-element.438), channel_id=1, source_target_pairs={{0,4},{4,8},{8,12},{12,16},{16,20},{20,24},{24,28},{28,32},{32,36}... | collective-permute-start | bytes 786440 | tf_op jit(solution)/shard_map/while/body/eval_jaxpr/ppermute | solution.py:17
  428.3 8.9 collective-permute-start
  438.4 9.5 %collective-permute-start = (bf16[2,256,256]{1,2,0:T(8,128)(2,1)S(1)}, bf16[2,256,256]{1,2,0:T(8,128)(2,1)S(1)}, u32[]{:S(2)}, u32[]{:S(2)}) collective-permute-start(bf16[2,256,256]{1,2,0:T(8,128)(2,1)S(1)} %get-tuple-element.438), channel_id=1, source_target_pairs={{0,4},{4,8},{8,12},{12,16},{16,20},{20,24},{24,28},{28,32},{32,36}... | collective-permute-start | bytes 786440 | tf_op jit(solution)/shard_map/while/body/eval_jaxpr/ppermute | solution.py:17
  449.1 9.6 %collective-permute-start = (bf16[2,256,256]{1,2,0:T(8,128)(2,1)S(1)}, bf16[2,256,256]{1,2,0:T(8,128)(2,1)S(1)}, u32[]{:S(2)}, u32[]{:S(2)}) collective-permute-start(bf16[2,256,256]{1,2,0:T(8,128)(2,1)S(1)} %get-tuple-element.438), channel_id=1, source_target_pairs={{0,4},{4,8},{8,12},{12,16},{16,20},{20,24},{24,28},{28,32},{32,36}... | collective-permute-start | bytes 786440 | tf_op jit(solution)/shard_map/while/body/eval_jaxpr/ppermute | solution.py:17
  459.8 10.4 %collective-permute-start = (bf16[2,256,256]{1,2,0:T(8,128)(2,1)S(1)}, bf16[2,256,256]{1,2,0:T(8,128)(2,1)S(1)}, u32[]{:S(2)}, u32[]{:S(2)}) collective-permute-start(bf16[2,256,256]{1,2,0:T(8,128)(2,1)S(1)} %get-tuple-element.438), channel_id=1, source_target_pairs={{0,4},{4,8},{8,12},{12,16},{16,20},{20,24},{24,28},{28,32},{32,36}... | collective-permute-start | bytes 786440 | tf_op jit(solution)/shard_map/while/body/eval_jaxpr/ppermute | solution.py:17
  471.3 11.5 %collective-permute-start = (bf16[2,256,256]{1,2,0:T(8,128)(2,1)S(1)}, bf16[2,256,256]{1,2,0:T(8,128)(2,1)S(1)}, u32[]{:S(2)}, u32[]{:S(2)}) collective-permute-start(bf16[2,256,256]{1,2,0:T(8,128)(2,1)S(1)} %get-tuple-element.438), channel_id=1, source_target_pairs={{0,4},{4,8},{8,12},{12,16},{16,20},{20,24},{24,28},{28,32},{32,36}... | collective-permute-start | bytes 786440 | tf_op jit(solution)/shard_map/while/body/eval_jaxpr/ppermute | solution.py:17
  484.0 12.7 %collective-permute-start = (bf16[2,256,256]{1,2,0:T(8,128)(2,1)S(1)}, bf16[2,256,256]{1,2,0:T(8,128)(2,1)S(1)}, u32[]{:S(2)}, u32[]{:S(2)}) collective-permute-start(bf16[2,256,256]{1,2,0:T(8,128)(2,1)S(1)} %get-tuple-element.438), channel_id=1, source_target_pairs={{0,4},{4,8},{8,12},{12,16},{16,20},{20,24},{24,28},{28,32},{32,36}... | collective-permute-start | bytes 786440 | tf_op jit(solution)/shard_map/while/body/eval_jaxpr/ppermute | solution.py:17
  497.9 9.6 %collective-permute-start = (bf16[2,256,256]{1,2,0:T(8,128)(2,1)S(1)}, bf16[2,256,256]{1,2,0:T(8,128)(2,1)S(1)}, u32[]{:S(2)}, u32[]{:S(2)}) collective-permute-start(bf16[2,256,256]{1,2,0:T(8,128)(2,1)S(1)} %get-tuple-element.438), channel_id=1, source_target_pairs={{0,4},{4,8},{8,12},{12,16},{16,20},{20,24},{24,28},{28,32},{32,36}... | collective-permute-start | bytes 786440 | tf_op jit(solution)/shard_map/while/body/eval_jaxpr/ppermute | solution.py:17
  508.6 9.0 collective-permute-start
  518.7 8.3 collective-permute-start
  528.1 11.1 %collective-permute-start = (bf16[2,256,256]{1,2,0:T(8,128)(2,1)S(1)}, bf16[2,256,256]{1,2,0:T(8,128)(2,1)S(1)}, u32[]{:S(2)}, u32[]{:S(2)}) collective-permute-start(bf16[2,256,256]{1,2,0:T(8,128)(2,1)S(1)} %get-tuple-element.438), channel_id=1, source_target_pairs={{0,4},{4,8},{8,12},{12,16},{16,20},{20,24},{24,28},{28,32},{32,36}... | collective-permute-start | bytes 786440 | tf_op jit(solution)/shard_map/while/body/eval_jaxpr/ppermute | solution.py:17
  540.4 16.1 %collective-permute-start = (bf16[2,256,256]{1,2,0:T(8,128)(2,1)S(1)}, bf16[2,256,256]{1,2,0:T(8,128)(2,1)S(1)}, u32[]{:S(2)}, u32[]{:S(2)}) collective-permute-start(bf16[2,256,256]{1,2,0:T(8,128)(2,1)S(1)} %get-tuple-element.438), channel_id=1, source_target_pairs={{0,4},{4,8},{8,12},{12,16},{16,20},{20,24},{24,28},{28,32},{32,36}... | collective-permute-start | bytes 786440 | tf_op jit(solution)/shard_map/while/body/eval_jaxpr/ppermute | solution.py:17
  557.6 9.3 %collective-permute-start = (bf16[2,256,256]{1,2,0:T(8,128)(2,1)S(1)}, bf16[2,256,256]{1,2,0:T(8,128)(2,1)S(1)}, u32[]{:S(2)}, u32[]{:S(2)}) collective-permute-start(bf16[2,256,256]{1,2,0:T(8,128)(2,1)S(1)} %get-tuple-element.438), channel_id=1, source_target_pairs={{0,4},{4,8},{8,12},{12,16},{16,20},{20,24},{24,28},{28,32},{32,36}... | collective-permute-start | bytes 786440 | tf_op jit(solution)/shard_map/while/body/eval_jaxpr/ppermute | solution.py:17
  568.1 11.7 %collective-permute-start = (bf16[2,256,256]{1,2,0:T(8,128)(2,1)S(1)}, bf16[2,256,256]{1,2,0:T(8,128)(2,1)S(1)}, u32[]{:S(2)}, u32[]{:S(2)}) collective-permute-start(bf16[2,256,256]{1,2,0:T(8,128)(2,1)S(1)} %get-tuple-element.438), channel_id=1, source_target_pairs={{0,4},{4,8},{8,12},{12,16},{16,20},{20,24},{24,28},{28,32},{32,36}... | collective-permute-start | bytes 786440 | tf_op jit(solution)/shard_map/while/body/eval_jaxpr/ppermute | solution.py:17
  580.9 10.4 %collective-permute-start = (bf16[2,256,256]{1,2,0:T(8,128)(2,1)S(1)}, bf16[2,256,256]{1,2,0:T(8,128)(2,1)S(1)}, u32[]{:S(2)}, u32[]{:S(2)}) collective-permute-start(bf16[2,256,256]{1,2,0:T(8,128)(2,1)S(1)} %get-tuple-element.438), channel_id=1, source_target_pairs={{0,4},{4,8},{8,12},{12,16},{16,20},{20,24},{24,28},{28,32},{32,36}... | collective-permute-start | bytes 786440 | tf_op jit(solution)/shard_map/while/body/eval_jaxpr/ppermute | solution.py:17
  592.5 10.7 %collective-permute-start = (bf16[2,256,256]{1,2,0:T(8,128)(2,1)S(1)}, bf16[2,256,256]{1,2,0:T(8,128)(2,1)S(1)}, u32[]{:S(2)}, u32[]{:S(2)}) collective-permute-start(bf16[2,256,256]{1,2,0:T(8,128)(2,1)S(1)} %get-tuple-element.438), channel_id=1, source_target_pairs={{0,4},{4,8},{8,12},{12,16},{16,20},{20,24},{24,28},{28,32},{32,36}... | collective-permute-start | bytes 786440 | tf_op jit(solution)/shard_map/while/body/eval_jaxpr/ppermute | solution.py:17
  604.3 10.6 %collective-permute-start = (bf16[2,256,256]{1,2,0:T(8,128)(2,1)S(1)}, bf16[2,256,256]{1,2,0:T(8,128)(2,1)S(1)}, u32[]{:S(2)}, u32[]{:S(2)}) collective-permute-start(bf16[2,256,256]{1,2,0:T(8,128)(2,1)S(1)} %get-tuple-element.438), channel_id=1, source_target_pairs={{0,4},{4,8},{8,12},{12,16},{16,20},{20,24},{24,28},{28,32},{32,36}... | collective-permute-start | bytes 786440 | tf_op jit(solution)/shard_map/while/body/eval_jaxpr/ppermute | solution.py:17
  616.1 9.7 %collective-permute-start = (bf16[2,256,256]{1,2,0:T(8,128)(2,1)S(1)}, bf16[2,256,256]{1,2,0:T(8,128)(2,1)S(1)}, u32[]{:S(2)}, u32[]{:S(2)}) collective-permute-start(bf16[2,256,256]{1,2,0:T(8,128)(2,1)S(1)} %get-tuple-element.438), channel_id=1, source_target_pairs={{0,4},{4,8},{8,12},{12,16},{16,20},{20,24},{24,28},{28,32},{32,36}... | collective-permute-start | bytes 786440 | tf_op jit(solution)/shard_map/while/body/eval_jaxpr/ppermute | solution.py:17
  626.9 10.1 %collective-permute-start = (bf16[2,256,256]{1,2,0:T(8,128)(2,1)S(1)}, bf16[2,256,256]{1,2,0:T(8,128)(2,1)S(1)}, u32[]{:S(2)}, u32[]{:S(2)}) collective-permute-start(bf16[2,256,256]{1,2,0:T(8,128)(2,1)S(1)} %get-tuple-element.438), channel_id=1, source_target_pairs={{0,4},{4,8},{8,12},{12,16},{16,20},{20,24},{24,28},{28,32},{32,36}... | collective-permute-start | bytes 786440 | tf_op jit(solution)/shard_map/while/body/eval_jaxpr/ppermute | solution.py:17
  638.2 10.7 %collective-permute-start = (bf16[2,256,256]{1,2,0:T(8,128)(2,1)S(1)}, bf16[2,256,256]{1,2,0:T(8,128)(2,1)S(1)}, u32[]{:S(2)}, u32[]{:S(2)}) collective-permute-start(bf16[2,256,256]{1,2,0:T(8,128)(2,1)S(1)} %get-tuple-element.438), channel_id=1, source_target_pairs={{0,4},{4,8},{8,12},{12,16},{16,20},{20,24},{24,28},{28,32},{32,36}... | collective-permute-start | bytes 786440 | tf_op jit(solution)/shard_map/while/body/eval_jaxpr/ppermute | solution.py:17
  650.0 10.1 %collective-permute-start = (bf16[2,256,256]{1,2,0:T(8,128)(2,1)S(1)}, bf16[2,256,256]{1,2,0:T(8,128)(2,1)S(1)}, u32[]{:S(2)}, u32[]{:S(2)}) collective-permute-start(bf16[2,256,256]{1,2,0:T(8,128)(2,1)S(1)} %get-tuple-element.438), channel_id=1, source_target_pairs={{0,4},{4,8},{8,12},{12,16},{16,20},{20,24},{24,28},{28,32},{32,36}... | collective-permute-start | bytes 786440 | tf_op jit(solution)/shard_map/while/body/eval_jaxpr/ppermute | solution.py:17
  661.2 11.1 %collective-permute-start = (bf16[2,256,256]{1,2,0:T(8,128)(2,1)S(1)}, bf16[2,256,256]{1,2,0:T(8,128)(2,1)S(1)}, u32[]{:S(2)}, u32[]{:S(2)}) collective-permute-start(bf16[2,256,256]{1,2,0:T(8,128)(2,1)S(1)} %get-tuple-element.438), channel_id=1, source_target_pairs={{0,4},{4,8},{8,12},{12,16},{16,20},{20,24},{24,28},{28,32},{32,36}... | collective-permute-start | bytes 786440 | tf_op jit(solution)/shard_map/while/body/eval_jaxpr/ppermute | solution.py:17
  673.5 13.5 %collective-permute-start = (bf16[2,256,256]{1,2,0:T(8,128)(2,1)S(1)}, bf16[2,256,256]{1,2,0:T(8,128)(2,1)S(1)}, u32[]{:S(2)}, u32[]{:S(2)}) collective-permute-start(bf16[2,256,256]{1,2,0:T(8,128)(2,1)S(1)} %get-tuple-element.438), channel_id=1, source_target_pairs={{0,4},{4,8},{8,12},{12,16},{16,20},{20,24},{24,28},{28,32},{32,36}... | collective-permute-start | bytes 786440 | tf_op jit(solution)/shard_map/while/body/eval_jaxpr/ppermute | solution.py:17
  688.1 13.1 %collective-permute-start = (bf16[2,256,256]{1,2,0:T(8,128)(2,1)S(1)}, bf16[2,256,256]{1,2,0:T(8,128)(2,1)S(1)}, u32[]{:S(2)}, u32[]{:S(2)}) collective-permute-start(bf16[2,256,256]{1,2,0:T(8,128)(2,1)S(1)} %get-tuple-element.438), channel_id=1, source_target_pairs={{0,4},{4,8},{8,12},{12,16},{16,20},{20,24},{24,28},{28,32},{32,36}... | collective-permute-start | bytes 786440 | tf_op jit(solution)/shard_map/while/body/eval_jaxpr/ppermute | solution.py:17
  702.4 10.4 %collective-permute-start = (bf16[2,256,256]{1,2,0:T(8,128)(2,1)S(1)}, bf16[2,256,256]{1,2,0:T(8,128)(2,1)S(1)}, u32[]{:S(2)}, u32[]{:S(2)}) collective-permute-start(bf16[2,256,256]{1,2,0:T(8,128)(2,1)S(1)} %get-tuple-element.438), channel_id=1, source_target_pairs={{0,4},{4,8},{8,12},{12,16},{16,20},{20,24},{24,28},{28,32},{32,36}... | collective-permute-start | bytes 786440 | tf_op jit(solution)/shard_map/while/body/eval_jaxpr/ppermute | solution.py:17
  (1 other events, 8.0 us)
Sparse Core Ops, SparseCore 0:
  720.1 171.1 reduce-scatter.1
where the time goes:
time: 901 us; the launch traced here: 898 us
  waiting for transfers between devices  395 us (44%)
  starting transfers between devices  379 us (42%)
  matrix products  61.4 us (7%)
  other arithmetic  33.9 us (4%)
  between operations  13.5 us (1%)
    ppermute x63, starting transfers between devices, from_behind(): return lax.ppermute(block, axis, route)  379 us
    ppermute x63, waiting for transfers between devices, from_behind(): return lax.ppermute(block, axis, route)  224 us
    reduce_scatter x1, waiting for transfers between devices, per_device(): lax.psum_scatter(jnp.dot(attended, out_weight, preferred_element_type=jnp...  171 us
    dot_general x64, matrix products, attend(): jnp.einsum('kgqs,skd->kgqd', rounded, v_heads, preferred_element_type=jnp...  31.5 us
    dot_general x64, matrix products, attend(): jnp.einsum('qkgd,skd->kgqs', q_heads, k_heads, preferred_element_type=jnp...  24.2 us
  transfers between devices with their start and end apart: 64, of which 64 were waited for; matrix products, arithmetic and copies ran while one was open for 2% of the time, Pallas kernels for 0%

commit v1 on v0

v1 whole, which is shorter than its diff:
```python
import functools

import jax
import jax.numpy as jnp
import numpy as np
from jax import lax
from jax.experimental import pallas as pl
from jax.experimental.pallas import tpu as pltpu
from jax.sharding import PartitionSpec as P

MESH = pl.DeviceIdType.MESH
HD = 128
T = 256
NY, NZ, NX = 4, 8, 2
D = 5376
CH = 768
NCH = D // CH
QSCALE = float(168.0 ** (-0.5) * np.log2(np.e))
NEG = -1e30


def kernel(
    q_ref, k_ref, v_ref, doc_ref, w_ref, o_ref,
    w_vm, qsrc, ksrc, kv, q_in, qt, m_s, l_s, acc, o_out, st_out, o_in, st_in,
    att, p_own, p_sib, sib_in, cut_out, cut_in,
    w_sem, a_kv_s, a_q_s, r_sem, f_sem, h_s, h_r, q_r, ot_s, ot_r, st_s, st_r,
    sb_s, sb_r, cu_s, cu_r,
):
    ctx, head = lax.axis_index("ctx"), lax.axis_index("head")
    y, z, x = ctx // 16, (ctx // 2) % 8, ctx % 2
    xh, c = head // 2, head % 2

    def dev(yy, zz, xx, cc, hh=xh):
        return {"ctx": (yy * 8 + zz) * 2 + xx, "head": hh * 2 + cc}

    def remote(src, dst, s, r, to):
        return pltpu.make_async_remote_copy(
            src_ref=src, dst_ref=dst, send_sem=s, recv_sem=r, device_id=to, device_id_type=MESH
        )

    barrier = pltpu.get_barrier_semaphore()

    def greet(to):
        pl.semaphore_signal(barrier, inc=1, device_id=to, device_id_type=MESH)

    for i in range(1, 16):
        greet(dev((y + i // 4) % 4, z, (x + (i // 2) % 2) % 2, (c + i) % 2))
    up, down = (z + 1) % 8, (z + 7) % 8
    greet(dev(y, up, x, c))
    greet(dev(y, down, x, c))
    greet(dev(y, z, x, c, 1 - xh))

    w_copy = pltpu.make_async_copy(w_ref, w_vm, w_sem)
    w_copy.start()

    for i in range(2):
        ksrc[0, i] = k_ref[:, i * HD:(i + 1) * HD]
        for t in range(2):
            part = v_ref[t * HD:(t + 1) * HD, i * HD:(i + 1) * HD]
            ksrc[1, i, t * HD:(t + 1) * HD, :] = part.astype(jnp.float32).T.astype(jnp.bfloat16)
    for j in range(4):
        part = q_ref[:, j * HD:(j + 1) * HD]
        qsrc[j] = part.astype(jnp.float32).T.astype(jnp.bfloat16)
    m_s[...] = jnp.full(m_s.shape, NEG, jnp.float32)
    l_s[...] = jnp.zeros(l_s.shape, jnp.float32)
    acc[...] = jnp.zeros(acc.shape, jnp.float32)

    pl.semaphore_wait(barrier, 18)

    def kv_copy(i, n):
        return remote(
            ksrc.at[n, i], kv.at[n, z, y], a_kv_s.at[n, i], r_sem.at[0, y], dev(2 * c + i, z, x, n)
        )

    def kv_self(i, n):
        return (2 * c + i == y) & (c == n)

    def q_copy(j, xx):
        return remote(
            qsrc.at[j], q_in.at[y, x], a_q_s.at[j, xx], q_r.at[y, x],
            dev(2 * c + j // 2, z, xx, j % 2),
        )

    def q_self(j, xx):
        return (2 * c + j // 2 == y) & (c == j % 2) & (xx == x)

    def either(cond, there, here):
        @pl.when(jnp.logical_not(cond))
        def _():
            there()

        if here is not None:

            @pl.when(cond)
            def _():
                here()

    for i in range(2):
        for n in range(2):
            either(
                kv_self(i, n),
                lambda i=i, n=n: kv_copy(i, n).start(),
                lambda i=i, n=n: pltpu.make_async_copy(
                    ksrc.at[n, i], kv.at[n, z, y], r_sem.at[0, y]
                ).start(),
            )
    for j in range(4):
        for xx in range(2):
            either(
                q_self(j, xx),
                lambda j=j, xx=xx: q_copy(j, xx).start(),
                lambda j=j, xx=xx: pltpu.make_async_copy(
                    qsrc.at[j], q_in.at[y, x], q_r.at[y, x]
                ).start(),
            )

    def place(s):
        dist = (s + 1) // 2
        return (z + 8 + jnp.where(s % 2 == 1, -dist, dist)) % 8

    def pass_on(s, yk, to_slot, to_z):
        zz = place(s)
        return remote(
            kv.at[c, zz, yk], kv.at[c, zz, yk], f_sem.at[to_slot, yk], r_sem.at[to_slot, yk],
            dev(y, to_z, x, c),
        )

    def share(s, yk):
        zz = place(s)
        return remote(
            kv.at[c, zz, yk], kv.at[c, zz, yk], h_s.at[s, yk], h_r.at[s, yk], dev(y, z, x, 1 - c)
        )

    def landed(ref, sem):
        pltpu.make_async_copy(ref, ref, sem).wait()

    def forwards(s, yk, act):
        @pl.when(s == 0)
        def _():
            act(pass_on(s, yk, 1, up))
            act(pass_on(s, yk, 2, down))

        @pl.when((s > 0) & (s < 5))
        def _():
            act(pass_on(s, yk, s + 2, jnp.where(s % 2 == 1, up, down)))

        @pl.when((s == 5) & (c == 0))
        def _():
            act(pass_on(s, yk, 7, up))

        @pl.when((s == 6) & (c == 1))
        def _():
            act(pass_on(s, yk, 7, down))

    def comm(e):
        s, yk = e // 4, (e + 3) % 4
        landed(kv.at[c, place(s), yk], r_sem.at[s, yk])
        forwards(s, yk, lambda copy: copy.start())
        share(s, yk).start()

    def attend(yq, zz, yk, masked):
        kb = kv[0, zz, yk]
        vb = kv[1, zz, yk]
        vt = jnp.concatenate([vb[:HD], vb[HD:]], axis=1)
        scores = jnp.dot(
            jnp.concatenate([kb, kb], axis=1), qt[yq], preferred_element_type=jnp.float32
        )
        if masked:
            row = lax.broadcasted_iota(jnp.int32, (T, 1), 0)
            col = lax.broadcasted_iota(jnp.int32, (1, 2 * T), 1)
            kbase, qbase = (16 * yk + 2 * zz + x) * 2, (16 * yq + 2 * z) * 2
            kdoc = jnp.where(row < HD, doc_ref[kbase], doc_ref[kbase + 1])
            qdoc = jnp.where(
                col < HD, doc_ref[qbase],
                jnp.where(
                    col < 2 * HD, doc_ref[qbase + 1],
                    jnp.where(col < 3 * HD, doc_ref[qbase + 2], doc_ref[qbase + 3]),
                ),
            )
            allowed = (kdoc == qdoc) & (row + kbase * HD <= col + qbase * HD)
            scores = jnp.where(allowed, scores, NEG)
        old = m_s[yq]
        new = jnp.maximum(old, jnp.max(scores, axis=0, keepdims=True))
        weights = jnp.exp2(scores - new)
        shrink = jnp.exp2(old - new)
        m_s[yq] = new
        l_s[yq] = l_s[yq] * shrink + jnp.sum(weights, axis=0, keepdims=True)
        acc[yq] = acc[yq] * shrink + jnp.dot(
            vt, weights.astype(jnp.bfloat16), preferred_element_type=jnp.float32
        )

    def compute(e):
        s, yk = e // 4, (e + 3) % 4
        zz = place(s)
        landed(kv.at[1 - c, zz, yk], h_r.at[s, yk])
        need_mask = (yk == 3) | (zz == z)

        def later(yq, _):
            attend(yq, zz, yk, False)
            return 0

        first = jnp.where((zz < z) & (yk < 3), yk, yk + 1)
        lax.fori_loop(first, 3, later, 0)

        @pl.when(need_mask & (zz <= z))
        def _():
            attend(yk, zz, yk, True)

    for e in range(4):
        comm(e)
    for yy in range(4):
        for xx in range(2):
            landed(q_in.at[yy, xx], q_r.at[yy, xx])
            scaled = q_in[yy, xx].astype(jnp.float32) * QSCALE
            hi = scaled.astype(jnp.bfloat16)
            qt[yy, :HD, xx * T:(xx + 1) * T] = hi
            qt[yy, HD:, xx * T:(xx + 1) * T] = (scaled - hi.astype(jnp.float32)).astype(jnp.bfloat16)

    def turn(e, _):
        @pl.when(e < 32)
        def _():
            comm(e)

        compute(e - 4)
        return 0

    lax.fori_loop(4, 36, turn, 0)

    def back(yy, xx):
        j = 2 * (y % 2) + c
        to = dev(yy, z, xx, y // 2)
        return (
            remote(o_out.at[yy, xx], o_in.at[x, j], ot_s.at[yy, xx], ot_r.at[x, j], to),
            remote(st_out.at[yy, xx], st_in.at[x, j], st_s.at[yy, xx], st_r.at[x, j], to),
        )

    def back_self(yy, xx):
        return (yy == y) & (xx == x) & (c == y // 2)

    def back_here(yy, xx):
        j = 2 * (y % 2) + c
        pltpu.make_async_copy(o_out.at[yy, xx], o_in.at[x, j], ot_r.at[x, j]).start()
        pltpu.make_async_copy(st_out.at[yy, xx], st_in.at[x, j], st_r.at[x, j]).start()

    for yy in (3, 0, 1, 2):
        part = acc[yy] / l_s[yy]
        for xx in range(2):
            lanes = slice(xx * T, (xx + 1) * T)
            o_out[yy, xx] = part[:, lanes].astype(jnp.bfloat16)
            st_out[yy, xx, 0:1] = m_s[yy][:, lanes]
            st_out[yy, xx, 1:2] = l_s[yy][:, lanes]
            st_out[yy, xx, 2:8] = jnp.zeros((6, T), jnp.float32)
            either(
                back_self(yy, xx),
                lambda yy=yy, xx=xx: [copy.start() for copy in back(yy, xx)],
                lambda yy=yy, xx=xx: back_here(yy, xx),
            )

    for j in range(4):
        for xx in range(2):
            landed(o_in.at[xx, j], ot_r.at[xx, j])
            landed(st_in.at[xx, j], st_r.at[xx, j])
        m0, m1 = st_in[0, j, 0:1], st_in[1, j, 0:1]
        peak = jnp.maximum(m0, m1)
        a0 = st_in[0, j, 1:2] * jnp.exp2(m0 - peak)
        a1 = st_in[1, j, 1:2] * jnp.exp2(m1 - peak)
        whole = a0 + a1
        merged = o_in[0, j].astype(jnp.float32) * (a0 / whole) + o_in[1, j].astype(jnp.float32) * (
            a1 / whole
        )
        att[:, j * HD:(j + 1) * HD] = merged.T.astype(jnp.bfloat16)

    w_copy.wait()

    def to_sib(n):
        return remote(p_sib.at[n], sib_in.at[n], sb_s.at[n], sb_r.at[n], dev(y, z, x, 1 - c))

    def to_cut(n):
        return remote(cut_out.at[n], cut_in.at[n], cu_s.at[n], cu_r.at[n], dev(y, z, x, c, 1 - xh))

    def project(n):
        cols = pl.ds(pl.multiple_of(n * CH, CH), CH)
        part = jnp.dot(att[...], w_vm[:, cols], preferred_element_type=jnp.float32)
        for h in range(4):
            rows = part[64 * h:64 * (h + 1)]

            @pl.when(c == h % 2)
            def _():
                p_own[n, h // 2] = rows

            @pl.when(c != h % 2)
            def _():
                p_sib[n, h // 2] = rows.astype(jnp.bfloat16)

        to_sib(n).start()

    def reduce_chip(n):
        to_sib(n).wait_recv()
        cut_out[n] = (p_own[n, 1 - xh] + sib_in[n, 1 - xh].astype(jnp.float32)).astype(jnp.bfloat16)
        to_cut(n).start()

    def proj_turn(n, _):
        @pl.when(n < NCH)
        def _():
            project(n)

        @pl.when(n > 0)
        def _():
            reduce_chip(n - 1)

        return 0

    lax.fori_loop(0, NCH + 1, proj_turn, 0)
    for n in range(NCH):
        to_cut(n).wait_recv()
        total = p_own[n, xh] + sib_in[n, xh].astype(jnp.float32) + cut_in[n].astype(jnp.float32)
        o_ref[:, n * CH:(n + 1) * CH] = total.astype(jnp.bfloat16)

    for i in range(2):
        for n in range(2):
            either(kv_self(i, n), lambda i=i, n=n: kv_copy(i, n).wait_send(), None)
    for j in range(4):
        for xx in range(2):
            either(q_self(j, xx), lambda j=j, xx=xx: q_copy(j, xx).wait_send(), None)

    def drain(e, _):
        s, yk = e // 4, (e + 3) % 4
        forwards(s, yk, lambda copy: copy.wait_send())
        share(s, yk).wait_send()
        return 0

    lax.fori_loop(0, 32, drain, 0)
    for yy in range(4):
        for xx in range(2):
            either(
                back_self(yy, xx),
                lambda yy=yy, xx=xx: [copy.wait_send() for copy in back(yy, xx)],
                None,
            )
    for n in range(NCH):
        to_sib(n).wait_send()
        to_cut(n).wait_send()


def per_device(queries, keys, values, doc_ids, out_weight):
    bf, f32 = jnp.bfloat16, jnp.float32
    vm, dma = pltpu.VMEM, pltpu.SemaphoreType.DMA
    scratch = [
        vm((512, D), bf),
        vm((4, HD, T), bf),
        vm((2, 2, T, HD), bf),
        vm((2, NZ, NY, T, HD), bf),
        vm((NY, NX, HD, T), bf),
        vm((NY, 2 * HD, 2 * T), bf),
        vm((NY, 1, 2 * T), f32),
        vm((NY, 1, 2 * T), f32),
        vm((NY, HD, 2 * T), f32),
        vm((NY, NX, HD, T), bf),
        vm((NY, NX, 8, T), f32),
        vm((NX, 4, HD, T), bf),
        vm((NX, 4, 8, T), f32),
        vm((T, 512), bf),
        vm((NCH, 2, 64, CH), f32),
        vm((NCH, 2, 64, CH), bf),
        vm((NCH, 2, 64, CH), bf),
        vm((NCH, 64, CH), bf),
        vm((NCH, 64, CH), bf),
        dma,
        dma((2, 2)),
        dma((4, 2)),
        dma((8, 4)),
        dma((8, 4)),
        dma((8, 4)),
        dma((8, 4)),
        dma((4, 2)),
        dma((4, 2)),
        dma((2, 4)),
        dma((4, 2)),
        dma((2, 4)),
        dma((NCH,)),
        dma((NCH,)),
        dma((NCH,)),
        dma((NCH,)),
    ]
    vmem = pl.BlockSpec(memory_space=pltpu.VMEM)
    return pl.pallas_call(
        kernel,
        out_shape=jax.ShapeDtypeStruct((64, D), bf),
        in_specs=[
            vmem, vmem, vmem,
            pl.BlockSpec(memory_space=pltpu.SMEM),
            pl.BlockSpec(memory_space=pl.ANY),
        ],
        out_specs=vmem,
        scratch_shapes=scratch,
        compiler_params=pltpu.CompilerParams(
            collective_id=0, has_side_effects=True, vmem_limit_bytes=48 * 2**20
        ),
    )(queries, keys, values, doc_ids, out_weight)


def solution(mesh):
    placed = (P("ctx", "head"), P("ctx", "head"), P("ctx", "head"), P(), P("head", None))
    return jax.shard_map(
        per_device, mesh=mesh, in_specs=placed, out_specs=P(("ctx", "head"), None), check_vma=False
    )
```

time: 901 us -> 83.2 us (0.09)
  the two profiles are of different devices: /device:TPU:1 before, /device:TPU:241 now
where the time goes in v1:
time: 83.2 us; the launch traced here: 83 us
  Pallas kernels  78.7 us (95%)
  local copies, waits for them, and re-layouts  4.26 us (5%)
    pallas_call x1, Pallas kernels, per_device(): pl.pallas_call(kernel, out_shape=jax.ShapeDtypeStruct((64, D), bf), in_sp...  78.7 us
    unnamed x9, local copies, waits for them, and re-layouts  4.26 us

profile of v1, /device:TPU:241, one launch (start us, length us, event | category | flops | bytes accessed | tf_op | source)
XLA Modules:
  0.0 83.0 jit_solution(9838542141345661473)
XLA Ops:
  0.0 0.0 copy-start
  0.0 0.9 %copy-done = bf16[256,512]{1,0:T(8,128)(2,1)S(1)} copy-done((bf16[256,512]{1,0:T(8,128)(2,1)S(1)}, bf16[256,512]{1,0:T(8,128)(2,1)}, u32[]{:S(2)}) %copy-start) | copy-done | bytes 262168
  1.0 0.0 copy-start.1
  1.0 0.9 %copy-done.1 = bf16[256,256]{1,0:T(8,128)(2,1)S(1)} copy-done((bf16[256,256]{1,0:T(8,128)(2,1)S(1)}, bf16[256,256]{1,0:T(8,128)(2,1)}, u32[]{:S(2)}) %copy-start.1) | copy-done | bytes 131096
  1.9 0.0 copy-start.2
  1.9 0.9 %copy-done.2 = bf16[256,256]{1,0:T(8,128)(2,1)S(1)} copy-done((bf16[256,256]{1,0:T(8,128)(2,1)S(1)}, bf16[256,256]{1,0:T(8,128)(2,1)}, u32[]{:S(2)}) %copy-start.2) | copy-done | bytes 131096
  2.8 0.0 copy-start.3
  2.8 0.7 copy-done.3
  3.4 78.7 %shard_map.55 = bf16[64,5376]{1,0:T(8,128)(2,1)S(1)} custom-call(bf16[256,512]{1,0:T(8,128)(2,1)S(1)} %copy-done, bf16[256,256]{1,0:T(8,128)(2,1)S(1)} %copy-done.1, bf16[256,256]{1,0:T(8,128)(2,1)S(1)} %copy-done.2, s32[128]{0:T(128)S(1)} %copy-done.3, bf16[512,5376]{1,0:T(8,128)(2,1)} %w_ref.1), custom_call_target="tpu_custom_call" | custom-call | tf_op jit(solution)/shard_map/pallas_call | solution.py:386
  82.2 0.8 %copy.7 = bf16[64,5376]{1,0:T(8,128)(2,1)} copy(bf16[64,5376]{1,0:T(8,128)(2,1)S(1)} %shard_map.55) | data formatting | bytes 1376256
Async XLA Ops:
  0.0 0.9 %copy-start = (bf16[256,512]{1,0:T(8,128)(2,1)S(1)}, bf16[256,512]{1,0:T(8,128)(2,1)}, u32[]{:S(2)}) copy-start(bf16[256,512]{1,0:T(8,128)(2,1)} %q_ref.1) | copy-start | bytes 786436
  1.0 0.9 %copy-start.1 = (bf16[256,256]{1,0:T(8,128)(2,1)S(1)}, bf16[256,256]{1,0:T(8,128)(2,1)}, u32[]{:S(2)}) copy-start(bf16[256,256]{1,0:T(8,128)(2,1)} %k_ref.1) | copy-start | bytes 393220
  1.9 0.9 %copy-start.2 = (bf16[256,256]{1,0:T(8,128)(2,1)S(1)}, bf16[256,256]{1,0:T(8,128)(2,1)}, u32[]{:S(2)}) copy-start(bf16[256,256]{1,0:T(8,128)(2,1)} %v_ref.1) | copy-start | bytes 393220
  2.8 0.7 copy-start.3

commit v2 on v1

v2 whole, which is shorter than its diff:
```python
import functools

import jax
import jax.numpy as jnp
import numpy as np
from jax import lax
from jax.experimental import pallas as pl
from jax.experimental.pallas import tpu as pltpu
from jax.sharding import PartitionSpec as P

MESH = pl.DeviceIdType.MESH
HD = 128
T = 256
NY, NZ, NX = 4, 8, 2
D = 5376
CH = 768
NCH = D // CH
QSCALE = float(168.0 ** (-0.5) * np.log2(np.e))
NEG = -1e30


def kernel(
    q_hbm, k_hbm, v_hbm, doc_hbm, w_ref, o_ref, q_ref, k_ref, v_ref, doc_ref,
    w_vm, qsrc, ksrc, kv, q_in, qt, m_s, l_s, acc, o_out, st_out, o_in, st_in,
    att, p_own, p_sib, sib_in, cut_out, cut_in,
    in_s, w_sem, a_kv_s, a_q_s, r_sem, f_sem, h_s, h_r, q_r, ot_s, ot_r, st_s, st_r,
    sb_s, sb_r, cu_s, cu_r,
):
    ctx, head = lax.axis_index("ctx"), lax.axis_index("head")
    y, z, x = ctx // 16, (ctx // 2) % 8, ctx % 2
    xh, c = head // 2, head % 2

    def dev(yy, zz, xx, cc, hh=xh):
        return {"ctx": (yy * 8 + zz) * 2 + xx, "head": hh * 2 + cc}

    def remote(src, dst, s, r, to):
        return pltpu.make_async_remote_copy(
            src_ref=src, dst_ref=dst, send_sem=s, recv_sem=r, device_id=to, device_id_type=MESH
        )

    loads = [
        pltpu.make_async_copy(src, dst, in_s.at[i])
        for i, (src, dst) in enumerate(
            ((q_hbm, q_ref), (k_hbm, k_ref), (v_hbm, v_ref), (doc_hbm, doc_ref))
        )
    ]
    for load in loads:
        load.start()
    barrier = pltpu.get_barrier_semaphore()

    def greet(to):
        pl.semaphore_signal(barrier, inc=1, device_id=to, device_id_type=MESH)

    for i in range(1, 16):
        greet(dev((y + i // 4) % 4, z, (x + (i // 2) % 2) % 2, (c + i) % 2))
    up, down = (z + 1) % 8, (z + 7) % 8
    greet(dev(y, up, x, c))
    greet(dev(y, down, x, c))
    greet(dev(y, z, x, c, 1 - xh))

    w_copy = pltpu.make_async_copy(w_ref, w_vm, w_sem)
    w_copy.start()

    for load in loads:
        load.wait()
    for i in range(2):
        ksrc[0, i] = k_ref[:, i * HD:(i + 1) * HD]
        for t in range(2):
            part = v_ref[t * HD:(t + 1) * HD, i * HD:(i + 1) * HD]
            ksrc[1, i, t * HD:(t + 1) * HD, :] = part.astype(jnp.float32).T.astype(jnp.bfloat16)
    for j in range(4):
        part = q_ref[:, j * HD:(j + 1) * HD]
        qsrc[j] = part.astype(jnp.float32).T.astype(jnp.bfloat16)
    m_s[...] = jnp.full(m_s.shape, NEG, jnp.float32)
    l_s[...] = jnp.zeros(l_s.shape, jnp.float32)
    acc[...] = jnp.zeros(acc.shape, jnp.float32)

    pl.semaphore_wait(barrier, 18)

    def kv_copy(i, n):
        return remote(
            ksrc.at[n, i], kv.at[n, z, y], a_kv_s.at[n, i], r_sem.at[0, y], dev(2 * c + i, z, x, n)
        )

    def kv_self(i, n):
        return (2 * c + i == y) & (c == n)

    def q_copy(j, xx):
        return remote(
            qsrc.at[j], q_in.at[y, x], a_q_s.at[j, xx], q_r.at[y, x],
            dev(2 * c + j // 2, z, xx, j % 2),
        )

    def q_self(j, xx):
        return (2 * c + j // 2 == y) & (c == j % 2) & (xx == x)

    def either(cond, there, here):
        @pl.when(jnp.logical_not(cond))
        def _():
            there()

        if here is not None:

            @pl.when(cond)
            def _():
                here()

    for i in range(2):
        for n in range(2):
            either(
                kv_self(i, n),
                lambda i=i, n=n: kv_copy(i, n).start(),
                lambda i=i, n=n: pltpu.make_async_copy(
                    ksrc.at[n, i], kv.at[n, z, y], r_sem.at[0, y]
                ).start(),
            )
    def place(s):
        dist = (s + 1) // 2
        return (z + 8 + jnp.where(s % 2 == 1, -dist, dist)) % 8

    def pass_on(s, yk, to_slot, to_z):
        zz = place(s)
        return remote(
            kv.at[c, zz, yk], kv.at[c, zz, yk], f_sem.at[to_slot, yk], r_sem.at[to_slot, yk],
            dev(y, to_z, x, c),
        )

    def share(s, yk):
        zz = place(s)
        return remote(
            kv.at[c, zz, yk], kv.at[c, zz, yk], h_s.at[s, yk], h_r.at[s, yk], dev(y, z, x, 1 - c)
        )

    def landed(ref, sem):
        pltpu.make_async_copy(ref, ref, sem).wait()

    def forwards(s, yk, act):
        @pl.when(s == 0)
        def _():
            act(pass_on(s, yk, 1, up))
            act(pass_on(s, yk, 2, down))

        @pl.when((s > 0) & (s < 5))
        def _():
            act(pass_on(s, yk, s + 2, jnp.where(s % 2 == 1, up, down)))

        @pl.when((s == 5) & (c == 0))
        def _():
            act(pass_on(s, yk, 7, up))

        @pl.when((s == 6) & (c == 1))
        def _():
            act(pass_on(s, yk, 7, down))

    order = (3, 0, 1, 2)

    def arrive(s, yk):
        landed(kv.at[c, place(s), yk], r_sem.at[s, yk])
        forwards(s, yk, lambda copy: copy.start())
        share(s, yk).start()

    def event(e, _):
        s, yk = 2 * (e // 4) + 1, (e + 3) % 4
        arrive(s, yk)

        @pl.when(s < 7)
        def _():
            arrive(s + 1, yk)

        return 0

    def scores_of(yq, zz, yk, masked):
        kb = kv[0, zz, yk]
        scores = jnp.dot(
            jnp.concatenate([kb, kb], axis=1), qt[yq], preferred_element_type=jnp.float32
        )
        if masked:
            row = lax.broadcasted_iota(jnp.int32, (T, 1), 0)
            col = lax.broadcasted_iota(jnp.int32, (1, 2 * T), 1)
            kbase, qbase = (16 * yk + 2 * zz + x) * 2, (16 * yq + 2 * z) * 2
            kdoc = jnp.where(row < HD, doc_ref[kbase], doc_ref[kbase + 1])
            qdoc = jnp.where(
                col < HD, doc_ref[qbase],
                jnp.where(
                    col < 2 * HD, doc_ref[qbase + 1],
                    jnp.where(col < 3 * HD, doc_ref[qbase + 2], doc_ref[qbase + 3]),
                ),
            )
            allowed = (kdoc == qdoc) & (row + kbase * HD <= col + qbase * HD)
            scores = jnp.where(allowed, scores, NEG)
        return scores

    def soften(yq, scores):
        old = m_s[yq]
        new = jnp.maximum(old, jnp.max(scores, axis=0, keepdims=True))
        m_s[yq] = new
        return jnp.exp2(scores - new).astype(jnp.bfloat16), jnp.exp2(old - new)

    def add_values(yq, zz, yk, weights, shrink):
        vb = kv[1, zz, yk]
        vt = jnp.concatenate([vb[:HD], vb[HD:]], axis=1)
        vt = jnp.concatenate([vt, jnp.ones((16, T), jnp.bfloat16)], axis=0)
        added = jnp.dot(vt, weights, preferred_element_type=jnp.float32)
        l_s[yq] = l_s[yq] * shrink + added[HD:HD + 1]
        acc[yq] = acc[yq] * shrink + added[:HD]

    def attend(zz, pieces):
        scores = [scores_of(yq, zz, yk, masked) for yq, yk, masked in pieces]
        soft = [soften(piece[0], one) for piece, one in zip(pieces, scores)]
        for (yq, yk, _), (weights, shrink) in zip(pieces, soft):
            add_values(yq, zz, yk, weights, shrink)

    before = [(2, 0, False), (1, 0, False), (2, 1, False)]

    def compute(s):
        zz = place(s)
        for yk in order:
            landed(kv.at[1 - c, zz, yk], h_r.at[s, yk])

        @pl.when(zz > z)
        def _():
            attend(zz, before)

        @pl.when(zz < z)
        def _():
            attend(zz, before + [(0, 0, False), (2, 2, False), (1, 1, False), (3, 3, True)])

        @pl.when(zz == z)
        def _():
            attend(zz, before + [(0, 0, True), (2, 2, True), (1, 1, True), (3, 3, True)])

    def send_queries():
        for j in range(4):
            for xx in range(2):
                either(
                    q_self(j, xx),
                    lambda j=j, xx=xx: q_copy(j, xx).start(),
                    lambda j=j, xx=xx: pltpu.make_async_copy(
                        qsrc.at[j], q_in.at[y, x], q_r.at[y, x]
                    ).start(),
                )

    for n, yk in enumerate(order):
        arrive(0, yk)
    send_queries()
    lax.fori_loop(0, 4, event, 0)
    for yy in range(4):
        for xx in range(2):
            landed(q_in.at[yy, xx], q_r.at[yy, xx])
            scaled = q_in[yy, xx].astype(jnp.float32) * QSCALE
            hi = scaled.astype(jnp.bfloat16)
            qt[yy, :HD, xx * T:(xx + 1) * T] = hi
            qt[yy, HD:, xx * T:(xx + 1) * T] = (scaled - hi.astype(jnp.float32)).astype(jnp.bfloat16)

    def seen(n):
        first = jnp.where(n < 1, 0, jnp.where(n < 5, n + 1, 8))
        return 4 + jnp.where(n < 6, first, jnp.where(n < 7, 9, 12))

    def turn(n, _):
        lax.fori_loop(jnp.where(n < 1, 4, seen(n - 1)), seen(n), event, 0)
        compute(n)
        return 0

    lax.fori_loop(0, 8, turn, 0)

    halves = (1 - xh, xh)

    def back(yy, xx, n):
        j = 2 * (y % 2) + c
        return remote(
            o_out.at[yy, xx, halves[n]], o_in.at[x, j, halves[n]],
            ot_s.at[n, yy, xx], ot_r.at[n, x, j], dev(yy, z, xx, y // 2),
        )

    def back_stats(yy, xx):
        j = 2 * (y % 2) + c
        return remote(
            st_out.at[yy, xx], st_in.at[x, j], st_s.at[yy, xx], st_r.at[x, j],
            dev(yy, z, xx, y // 2),
        )

    def back_self(yy, xx):
        return (yy == y) & (xx == x) & (c == y // 2)

    def back_here(yy, xx, n):
        j = 2 * (y % 2) + c
        pltpu.make_async_copy(
            o_out.at[yy, xx, halves[n]], o_in.at[x, j, halves[n]], ot_r.at[n, x, j]
        ).start()

    def back_stats_here(yy, xx):
        j = 2 * (y % 2) + c
        pltpu.make_async_copy(st_out.at[yy, xx], st_in.at[x, j], st_r.at[x, j]).start()

    def return_half(yy, xx, n):
        either(
            back_self(yy, xx),
            lambda: back(yy, xx, n).start(),
            lambda: back_here(yy, xx, n),
        )

    for yy in order:
        part = (acc[yy] * (1.0 / l_s[yy])).astype(jnp.bfloat16)
        for xx in range(2):
            for th in range(2):
                lanes = slice(xx * T + th * HD, xx * T + (th + 1) * HD)
                o_out[yy, xx, th] = part[:, lanes]
                st_out[yy, xx, th, 0:1] = m_s[yy][:, lanes]
                st_out[yy, xx, th, 1:2] = l_s[yy][:, lanes]
                st_out[yy, xx, th, 2:8] = jnp.zeros((6, HD), jnp.float32)
            either(
                back_self(yy, xx),
                lambda yy=yy, xx=xx: back_stats(yy, xx).start(),
                lambda yy=yy, xx=xx: back_stats_here(yy, xx),
            )
            return_half(yy, xx, 0)
    for yy in order:
        for xx in range(2):
            return_half(yy, xx, 1)

    def merge(n):
        for j in range(4):
            for xx in range(2):
                landed(o_in.at[xx, j, halves[n]], ot_r.at[n, xx, j])
                if n == 0:
                    landed(st_in.at[xx, j], st_r.at[xx, j])
            one, two = st_in[0, j, halves[n]], st_in[1, j, halves[n]]
            peak = jnp.maximum(one[0:1], two[0:1])
            a0 = one[1:2] * jnp.exp2(one[0:1] - peak)
            a1 = two[1:2] * jnp.exp2(two[0:1] - peak)
            whole = a0 + a1
            merged = o_in[0, j, halves[n]].astype(jnp.float32) * (a0 / whole) + o_in[
                1, j, halves[n]
            ].astype(jnp.float32) * (a1 / whole)
            att[n, :, j * HD:(j + 1) * HD] = merged.T.astype(jnp.bfloat16)

    def to_sib(h, n):
        return remote(
            p_sib.at[h, n], sib_in.at[h, n], sb_s.at[h, n], sb_r.at[h, n], dev(y, z, x, 1 - c)
        )

    def to_cut(n):
        return remote(cut_out.at[n], cut_in.at[n], cu_s.at[n], cu_r.at[n], dev(y, z, x, c, 1 - xh))

    def project(h, n):
        cols = pl.ds(pl.multiple_of(n * CH, CH), CH)
        part = jnp.dot(att[h], w_vm[:, cols], preferred_element_type=jnp.float32)

        @pl.when(c == 0)
        def _():
            p_own[h, n] = part[:64]
            p_sib[h, n] = part[64:].astype(jnp.bfloat16)

        @pl.when(c == 1)
        def _():
            p_own[h, n] = part[64:]
            p_sib[h, n] = part[:64].astype(jnp.bfloat16)

        to_sib(h, n).start()

    def reduce_chip(n):
        to_sib(0, n).wait_recv()
        cut_out[n] = (p_own[0, n] + sib_in[0, n].astype(jnp.float32)).astype(jnp.bfloat16)
        to_cut(n).start()

    def first_turn(n, _):
        @pl.when(n < NCH)
        def _():
            project(0, n)

        @pl.when(n > 0)
        def _():
            reduce_chip(n - 1)

        return 0

    def second_turn(n, _):
        project(1, n)
        return 0

    merge(0)
    w_copy.wait()
    lax.fori_loop(0, NCH + 1, first_turn, 0)
    merge(1)
    lax.fori_loop(0, NCH, second_turn, 0)
    for n in range(NCH):
        to_sib(1, n).wait_recv()
        p_own[1, n] = p_own[1, n] + sib_in[1, n].astype(jnp.float32)
    for n in range(NCH):
        to_cut(n).wait_recv()
        total = p_own[1, n] + cut_in[n].astype(jnp.float32)
        o_ref[:, n * CH:(n + 1) * CH] = total.astype(jnp.bfloat16)

    for i in range(2):
        for n in range(2):
            either(kv_self(i, n), lambda i=i, n=n: kv_copy(i, n).wait_send(), None)
    for j in range(4):
        for xx in range(2):
            either(q_self(j, xx), lambda j=j, xx=xx: q_copy(j, xx).wait_send(), None)

    for yk in order:
        forwards(0, yk, lambda copy: copy.wait_send())
    for yk in order:
        share(0, yk).wait_send()

    def drain(s, _):
        for yk in order:
            forwards(s, yk, lambda copy: copy.wait_send())
            share(s, yk).wait_send()
        return 0

    lax.fori_loop(1, 8, drain, 0)
    for yy in range(4):
        for xx in range(2):
            either(
                back_self(yy, xx),
                lambda yy=yy, xx=xx: [
                    copy.wait_send()
                    for copy in (back_stats(yy, xx), back(yy, xx, 0), back(yy, xx, 1))
                ],
                None,
            )
    for n in range(NCH):
        to_sib(0, n).wait_send()
        to_sib(1, n).wait_send()
        to_cut(n).wait_send()


def per_device(queries, keys, values, doc_ids, out_weight):
    bf, f32 = jnp.bfloat16, jnp.float32
    vm, dma = pltpu.VMEM, pltpu.SemaphoreType.DMA
    scratch = [
        vm((T, 512), bf),
        vm((T, 256), bf),
        vm((T, 256), bf),
        pltpu.SMEM((128,), jnp.int32),
        vm((512, D), bf),
        vm((4, HD, T), bf),
        vm((2, 2, T, HD), bf),
        vm((2, NZ, NY, T, HD), bf),
        vm((NY, NX, HD, T), bf),
        vm((NY, 2 * HD, 2 * T), bf),
        vm((NY, 1, 2 * T), f32),
        vm((NY, 1, 2 * T), f32),
        vm((NY, HD, 2 * T), f32),
        vm((NY, NX, 2, HD, HD), bf),
        vm((NY, NX, 2, 8, HD), f32),
        vm((NX, 4, 2, HD, HD), bf),
        vm((NX, 4, 2, 8, HD), f32),
        vm((2, HD, 512), bf),
        vm((2, NCH, 64, CH), f32),
        vm((2, NCH, 64, CH), bf),
        vm((2, NCH, 64, CH), bf),
        vm((NCH, 64, CH), bf),
        vm((NCH, 64, CH), bf),
        dma((4,)),
        dma,
        dma((2, 2)),
        dma((4, 2)),
        dma((8, 4)),
        dma((8, 4)),
        dma((8, 4)),
        dma((8, 4)),
        dma((4, 2)),
        dma((2, 4, 2)),
        dma((2, 2, 4)),
        dma((4, 2)),
        dma((2, 4)),
        dma((2, NCH)),
        dma((2, NCH)),
        dma((NCH,)),
        dma((NCH,)),
    ]
    vmem = pl.BlockSpec(memory_space=pltpu.VMEM)
    return pl.pallas_call(
        kernel,
        out_shape=jax.ShapeDtypeStruct((64, D), bf),
        in_specs=[pl.BlockSpec(memory_space=pltpu.HBM)] * 5,
        out_specs=vmem,
        scratch_shapes=scratch,
        compiler_params=pltpu.CompilerParams(
            collective_id=0, has_side_effects=True, vmem_limit_bytes=64 * 2**20
        ),
    )(queries, keys, values, doc_ids, out_weight)


def solution(mesh):
    placed = (P("ctx", "head"), P("ctx", "head"), P("ctx", "head"), P(), P("head", None))
    return jax.shard_map(
        per_device, mesh=mesh, in_specs=placed, out_specs=P(("ctx", "head"), None), check_vma=False
    )
```

time: 83.2 us -> 69.7 us (0.84)
  the two profiles are of different devices: /device:TPU:241 before, /device:TPU:1 now
where the time goes in v2:
time: 69.7 us; the launch traced here: 68.6 us
  Pallas kernels  66.6 us (96%)
  local copies, waits for them, and re-layouts  1.99 us (3%)
    pallas_call x1, Pallas kernels, per_device(): pl.pallas_call(kernel, out_shape=jax.ShapeDtypeStruct((64, D), bf), in_sp...  66.6 us
    unnamed x1, local copies, waits for them, and re-layouts  1.99 us

profile of v2, /device:TPU:1, one launch (start us, length us, event | category | flops | bytes accessed | tf_op | source)
XLA Modules:
  0.0 68.6 jit_solution(15335499580255578211)
XLA Ops:
  0.0 66.6 %shard_map.55 = bf16[64,5376]{1,0:T(8,128)(2,1)} custom-call(bf16[256,512]{1,0:T(8,128)(2,1)} %q_hbm.1, bf16[256,256]{1,0:T(8,128)(2,1)} %k_hbm.1, bf16[256,256]{1,0:T(8,128)(2,1)} %v_hbm.1, s32[128]{0:T(128)} %doc_hbm.1, bf16[512,5376]{1,0:T(8,128)(2,1)} %w_ref.1), custom_call_target="tpu_custom_call" | custom-call | tf_op jit(solution)/shard_map/pallas_call | solution.py:475
  66.6 2.0 %copy.7 = bf16[64,5376]{1,0:T(8,128)(2,1)} copy(bf16[64,5376]{1,0:T(8,128)(2,1)} %shard_map.55) | data formatting | bytes 1376256

commit v3 on v2

--- a/solution.py
+++ b/solution.py
@@ -22,8 +22,8 @@
 def kernel(
     q_hbm, k_hbm, v_hbm, doc_hbm, w_ref, o_ref, q_ref, k_ref, v_ref, doc_ref,
     w_vm, qsrc, ksrc, kv, q_in, qt, m_s, l_s, acc, o_out, st_out, o_in, st_in,
-    att, p_own, p_sib, sib_in, cut_out, cut_in,
-    in_s, w_sem, a_kv_s, a_q_s, r_sem, f_sem, h_s, h_r, q_r, ot_s, ot_r, st_s, st_r,
+    att, p_own, p_sib, sib_in, cut_out, cut_in, out_vm,
+    in_s, out_s, w_sem, a_kv_s, a_q_s, r_sem, f_sem, h_s, h_r, q_r, ot_s, ot_r, st_s, st_r,
     sb_s, sb_r, cu_s, cu_r,
 ):
     ctx, head = lax.axis_index("ctx"), lax.axis_index("head")
@@ -159,8 +159,12 @@
         forwards(s, yk, lambda copy: copy.start())
         share(s, yk).start()
 
+    def chunk(n):
+        return (y + n + (n == 2) * 1 - (n == 3) * 1) % 4
+
     def event(e, _):
-        s, yk = 2 * (e // 4) + 1, (e + 3) % 4
+        n = e % 4
+        s, yk = 2 * (e // 4) + 1, (y + n + jnp.where(n == 2, 1, jnp.where(n == 3, -1, 0))) % 4
         arrive(s, yk)
 
         @pl.when(s < 7)
@@ -240,8 +244,8 @@
                     ).start(),
                 )
 
-    for n, yk in enumerate(order):
-        arrive(0, yk)
+    for n in range(4):
+        arrive(0, chunk(n))
     send_queries()
     lax.fori_loop(0, 4, event, 0)
     for yy in range(4):
@@ -378,6 +382,9 @@
         project(1, n)
         return 0
 
+    def out_copy(n):
+        return pltpu.make_async_copy(out_vm.at[n], o_ref.at[:, n * CH:(n + 1) * CH], out_s.at[n])
+
     merge(0)
     w_copy.wait()
     lax.fori_loop(0, NCH + 1, first_turn, 0)
@@ -386,11 +393,6 @@
     for n in range(NCH):
         to_sib(1, n).wait_recv()
         p_own[1, n] = p_own[1, n] + sib_in[1, n].astype(jnp.float32)
-    for n in range(NCH):
-        to_cut(n).wait_recv()
-        total = p_own[1, n] + cut_in[n].astype(jnp.float32)
-        o_ref[:, n * CH:(n + 1) * CH] = total.astype(jnp.bfloat16)
-
     for i in range(2):
         for n in range(2):
             either(kv_self(i, n), lambda i=i, n=n: kv_copy(i, n).wait_send(), None)
@@ -420,7 +422,14 @@
                 ],
                 None,
             )
+
     for n in range(NCH):
+        to_cut(n).wait_recv()
+        total = p_own[1, n] + cut_in[n].astype(jnp.float32)
+        out_vm[n] = total.astype(jnp.bfloat16)
+        out_copy(n).start()
+    for n in range(NCH):
+        out_copy(n).wait()
         to_sib(0, n).wait_send()
         to_sib(1, n).wait_send()
         to_cut(n).wait_send()
@@ -453,7 +462,9 @@
         vm((2, NCH, 64, CH), bf),
         vm((NCH, 64, CH), bf),
         vm((NCH, 64, CH), bf),
+        vm((NCH, 64, CH), bf),
         dma((4,)),
+        dma((NCH,)),
         dma,
         dma((2, 2)),
         dma((4, 2)),
@@ -471,12 +482,11 @@
         dma((NCH,)),
         dma((NCH,)),
     ]
-    vmem = pl.BlockSpec(memory_space=pltpu.VMEM)
     return pl.pallas_call(
         kernel,
         out_shape=jax.ShapeDtypeStruct((64, D), bf),
         in_specs=[pl.BlockSpec(memory_space=pltpu.HBM)] * 5,
-        out_specs=vmem,
+        out_specs=pl.BlockSpec(memory_space=pltpu.HBM),
         scratch_shapes=scratch,
         compiler_params=pltpu.CompilerParams(
             collective_id=0, has_side_effects=True, vmem_limit_bytes=64 * 2**20

time: 69.7 us -> 68.1 us (0.977); the launches traced: 68.6 us -> 68 us
  no operation moved by 1% of the time
where the time goes in v3:
time: 68.1 us; the launch traced here: 68 us
  Pallas kernels  66 us (97%)
  local copies, waits for them, and re-layouts  1.99 us (3%)
    pallas_call x1, Pallas kernels, per_device(): pl.pallas_call(kernel, out_shape=jax.ShapeDtypeStruct((64, D), bf), in_sp...  66 us
    unnamed x1, local copies, waits for them, and re-layouts  1.99 us

profile of v3, /device:TPU:1, one launch (start us, length us, event | category | flops | bytes accessed | tf_op | source)
XLA Modules:
  0.0 68.0 jit_solution(11440483308052066555)
XLA Ops:
  0.0 66.0 %shard_map.55 = bf16[64,5376]{1,0:T(8,128)(2,1)} custom-call(bf16[256,512]{1,0:T(8,128)(2,1)} %q_hbm.1, bf16[256,256]{1,0:T(8,128)(2,1)} %k_hbm.1, bf16[256,256]{1,0:T(8,128)(2,1)} %v_hbm.1, s32[128]{0:T(128)} %doc_hbm.1, bf16[512,5376]{1,0:T(8,128)(2,1)} %w_ref.1), custom_call_target="tpu_custom_call" | custom-call | tf_op jit(solution)/shard_map/pallas_call | solution.py:485
  66.0 2.0 %copy.7 = bf16[64,5376]{1,0:T(8,128)(2,1)} copy(bf16[64,5376]{1,0:T(8,128)(2,1)} %shard_map.55) | data formatting | bytes 1376256

commit v4 on v3

--- a/solution.py
+++ b/solution.py
@@ -257,8 +257,7 @@
             qt[yy, HD:, xx * T:(xx + 1) * T] = (scaled - hi.astype(jnp.float32)).astype(jnp.bfloat16)
 
     def seen(n):
-        first = jnp.where(n < 1, 0, jnp.where(n < 5, n + 1, 8))
-        return 4 + jnp.where(n < 6, first, jnp.where(n < 7, 9, 12))
+        return 4 + n + jnp.where(n < 3, 2, jnp.where(n < 4, 3, jnp.where(n < 7, 4, 5)))
 
     def turn(n, _):
         lax.fori_loop(jnp.where(n < 1, 4, seen(n - 1)), seen(n), event, 0)
@@ -303,7 +302,7 @@
             lambda: back_here(yy, xx, n),
         )
 
-    for yy in order:
+    for yy in map(chunk, (3, 1, 2, 0)):
         part = (acc[yy] * (1.0 / l_s[yy])).astype(jnp.bfloat16)
         for xx in range(2):
             for th in range(2):
@@ -318,7 +317,7 @@
                 lambda yy=yy, xx=xx: back_stats_here(yy, xx),
             )
             return_half(yy, xx, 0)
-    for yy in order:
+    for yy in map(chunk, (3, 1, 2, 0)):
         for xx in range(2):
             return_half(yy, xx, 1)
 

time: 68.1 us -> 66.8 us (0.981)
  Pallas kernels: 66 us -> 64.6 us
    pallas_call x1, Pallas kernels: 66 us -> 64.6 us  [per_device(): pl.pallas_call(kernel, out_shape=jax.ShapeDtypeStruct((64, D), bf), in_sp...]
where the time goes in v4:
time: 66.8 us; the launch traced here: 66.6 us
  Pallas kernels  64.6 us (97%)
  local copies, waits for them, and re-layouts  1.99 us (3%)
    pallas_call x1, Pallas kernels, per_device(): pl.pallas_call(kernel, out_shape=jax.ShapeDtypeStruct((64, D), bf), in_sp...  64.6 us
    unnamed x1, local copies, waits for them, and re-layouts  1.99 us

profile of v4, /device:TPU:1, one launch (start us, length us, event | category | flops | bytes accessed | tf_op | source)
XLA Modules:
  0.0 66.6 jit_solution(11641670471523131890)
XLA Ops:
  0.0 64.6 %shard_map.55 = bf16[64,5376]{1,0:T(8,128)(2,1)} custom-call(bf16[256,512]{1,0:T(8,128)(2,1)} %q_hbm.1, bf16[256,256]{1,0:T(8,128)(2,1)} %k_hbm.1, bf16[256,256]{1,0:T(8,128)(2,1)} %v_hbm.1, s32[128]{0:T(128)} %doc_hbm.1, bf16[512,5376]{1,0:T(8,128)(2,1)} %w_ref.1), custom_call_target="tpu_custom_call" | custom-call | tf_op jit(solution)/shard_map/pallas_call | solution.py:484
  64.6 2.0 %copy.7 = bf16[64,5376]{1,0:T(8,128)(2,1)} copy(bf16[64,5376]{1,0:T(8,128)(2,1)} %shard_map.55) | data formatting | bytes 1376256

commit v5 on v4

--- a/solution.py
+++ b/solution.py
@@ -131,6 +131,9 @@
             kv.at[c, zz, yk], kv.at[c, zz, yk], h_s.at[s, yk], h_r.at[s, yk], dev(y, z, x, 1 - c)
         )
 
+    def used(s, yk):
+        return (yk < 2) | (place(s) <= z)
+
     def landed(ref, sem):
         pltpu.make_async_copy(ref, ref, sem).wait()
 
@@ -157,7 +160,10 @@
     def arrive(s, yk):
         landed(kv.at[c, place(s), yk], r_sem.at[s, yk])
         forwards(s, yk, lambda copy: copy.start())
-        share(s, yk).start()
+
+        @pl.when(used(s, yk))
+        def _():
+            share(s, yk).start()
 
     def chunk(n):
         return (y + n + (n == 2) * 1 - (n == 3) * 1) % 4
@@ -219,7 +225,10 @@
     def compute(s):
         zz = place(s)
         for yk in order:
-            landed(kv.at[1 - c, zz, yk], h_r.at[s, yk])
+
+            @pl.when(used(s, yk))
+            def _(yk=yk):
+                landed(kv.at[1 - c, zz, yk], h_r.at[s, yk])
 
         @pl.when(zz > z)
         def _():
@@ -407,7 +416,11 @@
     def drain(s, _):
         for yk in order:
             forwards(s, yk, lambda copy: copy.wait_send())
-            share(s, yk).wait_send()
+
+            @pl.when(used(s, yk))
+            def _(yk=yk):
+                share(s, yk).wait_send()
+
         return 0
 
     lax.fori_loop(1, 8, drain, 0)

time: 66.8 us -> 66.6 us (level)
  no operation moved by 1% of the time
where the time goes in v5:
time: 66.6 us; the launch traced here: 66.5 us
  Pallas kernels  64.5 us (97%)
  local copies, waits for them, and re-layouts  1.99 us (3%)
    pallas_call x1, Pallas kernels, per_device(): pl.pallas_call(kernel, out_shape=jax.ShapeDtypeStruct((64, D), bf), in_sp...  64.5 us
    unnamed x1, local copies, waits for them, and re-layouts  1.99 us

profile of v5, /device:TPU:1, one launch (start us, length us, event | category | flops | bytes accessed | tf_op | source)
XLA Modules:
  0.0 66.5 jit_solution(16368649022336348901)
XLA Ops:
  0.0 64.5 %shard_map.55 = bf16[64,5376]{1,0:T(8,128)(2,1)} custom-call(bf16[256,512]{1,0:T(8,128)(2,1)} %q_hbm.1, bf16[256,256]{1,0:T(8,128)(2,1)} %k_hbm.1, bf16[256,256]{1,0:T(8,128)(2,1)} %v_hbm.1, s32[128]{0:T(128)} %doc_hbm.1, bf16[512,5376]{1,0:T(8,128)(2,1)} %w_ref.1), custom_call_target="tpu_custom_call" | custom-call | tf_op jit(solution)/shard_map/pallas_call | solution.py:497
  64.5 2.0 %copy.7 = bf16[64,5376]{1,0:T(8,128)(2,1)} copy(bf16[64,5376]{1,0:T(8,128)(2,1)} %shard_map.55) | data formatting | bytes 1376256
